TPU v7x, 32 devices: a whole 2x2x4 slice. The times are simulated.
32 devices in a mesh: groups: 2 (over x), gx: 8 (over z, y), gy: 2 (over core).
Axes of the slice: x: 2, y: 2, z: 4, core: 2. Of those that a mesh axis runs over, the one named last changes fastest.
Arguments:
- field: float32 [128, 128, 1024], P(('groups', 'gx'), 'gy'), parts along dimension 0, may hold values from -6 to 6
- spectral: float32 [2, 32, 2, 32, 8192], P(None, 'gx', None, 'gy'), may hold values from -6 to 6
- mixing: float32 [2, 16, 16], replicated, may hold values from -1.5 to 1.5
- bias: float32 [2, 16], replicated, may hold values from -3 to 3
Outputs:
- result: float32 [128, 128, 1024], P(('groups', 'gx'), 'gy'), parts along dimension 0
There are 2 independent parts, one for each index of `groups`. A program takes and returns all parts, laid end to end along the dimension named above; an argument that names none is the same for every part. Nothing has to cross between parts.
All inputs are finite; a program needn't handle non-finite values.
Results may differ from a plain program's by a relative error of at most 0.0001.
Values sent between devices are 32-bit elements; how exact they have to be, the bound alone decides.
A program may use at most 192 MiB of HBM per device.

v0:
```python
import math

import jax
import jax.numpy as jnp
from jax import lax
from jax.sharding import PartitionSpec as P

C = 16
MX = 32
MY = 32
MZ = 32
NZ = 64
LAYERS = 2


def contract(form, left, right):
    return jnp.einsum(form, left, right, precision=lax.Precision.HIGHEST)


def signed_modes(count):
    half = count // 2
    return jnp.concatenate(
        [jnp.arange(half, dtype=jnp.int32), jnp.arange(half, dtype=jnp.int32) - half]
    )


def phase(frequencies, positions, length):
    turns = jnp.mod(frequencies[:, None] * positions[None, :], length).astype(jnp.float32)
    angle = turns * (2.0 * math.pi / length)
    return (jnp.cos(angle), jnp.sin(angle))


def reduce_y(partial_value):
    return lax.psum_scatter(partial_value, "gy", scatter_dimension=2, tiled=True)


def shards(field, spectral, mixing, bias):
    cells_x = field.shape[0]
    cells_y = field.shape[1]
    span_x = cells_x * lax.axis_size("gx")
    span_y = cells_y * lax.axis_size("gy")
    x_cells = lax.axis_index("gx") * cells_x + jnp.arange(cells_x, dtype=jnp.int32)
    y_cells = lax.axis_index("gy") * cells_y + jnp.arange(cells_y, dtype=jnp.int32)
    owned_x = spectral.shape[1]
    width = MZ * C
    x_modes = signed_modes(MX)
    y_modes = signed_modes(MY)
    z_cosine, z_sine = phase(jnp.arange(MZ, dtype=jnp.int32), jnp.arange(NZ, dtype=jnp.int32), NZ)
    z_weights = jnp.where(jnp.arange(MZ) == 0, 1.0, 2.0).astype(jnp.float32) / (
        span_x * span_y * NZ
    )
    back_cosine = z_cosine * z_weights[:, None]
    back_sine = z_sine * z_weights[:, None]
    y_cosine, y_sine = phase(y_modes, y_cells, span_y)

    def x_forward(blocks, frequencies):
        cosine, sine = phase(frequencies, x_cells, span_x)
        real = contract("xqk,px->pqk", blocks[:, 0], cosine) + contract(
            "xqk,px->pqk", blocks[:, 1], sine
        )
        imaginary = contract("xqk,px->pqk", blocks[:, 1], cosine) - contract(
            "xqk,px->pqk", blocks[:, 0], sine
        )
        return jnp.stack([real, imaginary], 1)

    def y_backward(blocks, frequencies):
        cosine, sine = phase(frequencies, y_cells, span_y)
        real = contract("xqk,qy->xyk", blocks[:, 0], cosine) - contract(
            "xqk,qy->xyk", blocks[:, 1], sine
        )
        imaginary = contract("xqk,qy->xyk", blocks[:, 1], cosine) + contract(
            "xqk,qy->xyk", blocks[:, 0], sine
        )
        return jnp.stack([real, imaginary], 1)

    signal = field.reshape(cells_x, cells_y, NZ, C)
    for layer in range(LAYERS):
        z_real = contract("xyzc,kz->xykc", signal, z_cosine)
        z_imaginary = -contract("xyzc,kz->xykc", signal, z_sine)
        y_real = contract("xykc,qy->xqkc", z_real, y_cosine) + contract(
            "xykc,qy->xqkc", z_imaginary, y_sine
        )
        y_imaginary = contract("xykc,qy->xqkc", z_imaginary, y_cosine) - contract(
            "xykc,qy->xqkc", z_real, y_sine
        )
        partial_y = jnp.stack([y_real, y_imaginary], 1).reshape(cells_x, 2, MY, width)

        def term_first(start, count, partial_y=partial_y):
            return x_forward(partial_y, x_modes)

        whole_y = lax.psum_scatter(
            term_first(jnp.int32(0), lax.axis_size("gx") * owned_x),
            "gx",
            scatter_dimension=0,
            tiled=True,
        )
        owned = reduce_y(whole_y)
        weights = spectral[layer]
        kept_y = owned.shape[2]
        tensor = weights.reshape(owned_x, 2, kept_y, MZ, C, C)
        modes = owned.reshape(owned_x, 2, kept_y, MZ, C)
        mixed_real = contract("pqkc,pqkco->pqko", modes[:, 0], tensor[:, 0]) - contract(
            "pqkc,pqkco->pqko", modes[:, 1], tensor[:, 1]
        )
        mixed_imaginary = contract("pqkc,pqkco->pqko", modes[:, 0], tensor[:, 1]) + contract(
            "pqkc,pqkco->pqko", modes[:, 1], tensor[:, 0]
        )
        mixed = jnp.stack([mixed_real, mixed_imaginary], 1).reshape(owned_x, 2, kept_y, width)
        add_piece = lax.all_gather(mixed, "gx", axis=0, tiled=True)
        add_cosine, add_sine = phase(x_modes, x_cells, span_x)
        add_real = contract("pqk,px->xqk", add_piece[:, 0], add_cosine) - contract(
            "pqk,px->xqk", add_piece[:, 1], add_sine
        )
        add_imaginary = contract("pqk,px->xqk", add_piece[:, 1], add_cosine) + contract(
            "pqk,px->xqk", add_piece[:, 0], add_sine
        )
        back_x = jnp.stack([add_real, add_imaginary], 1)
        back_y = y_backward(lax.all_gather(back_x, "gy", axis=2, tiled=True), y_modes)
        halves = back_y.reshape(cells_x, 2, cells_y, MZ, C)
        spatial = contract("xyko,kz->xyzo", halves[:, 0], back_cosine) - contract(
            "xyko,kz->xyzo", halves[:, 1], back_sine
        )
        local = contract("xyzc,co->xyzo", signal, mixing[layer]) + bias[layer]
        signal = jax.nn.gelu(spatial + local, approximate=False)
    return signal.reshape(cells_x, cells_y, NZ * C)


def solution(mesh):
    placed = (P(("groups", "gx"), "gy", None), P(None, "gx", None, "gy", None), P(), P())
    return jax.shard_map(
        shards,
        mesh=mesh,
        in_specs=placed,
        out_specs=P(("groups", "gx"), "gy", None),
        check_vma=False,
    )
```

profile of v0, /device:TPU:0, one launch (start us, length us, event | category | flops | bytes accessed | tf_op | source)
XLA Modules:
  0.0 782.3 jit_solution(7077586470305244862)
XLA Ops:
  15.9 13.8 %fusion.95 = f32[32,8,64,16]{2,0,3,1:T(8,128)S(1)} fusion(f32[8,64,64,16]{2,1,3,0:T(8,128)} %copy.75), kind=kOutput, calls=%fused_computation.151 | convolution fusion | flops 201355264 | bytes 3145728 | tf_op jit(solution)/shard_map/xyzc,kz->xykc/dot_general | solution.py:17
  29.8 12.8 %fusion.107 = f32[32,8,64,16]{2,0,3,1:T(8,128)} fusion(f32[8,64,64,16]{2,1,3,0:T(8,128)S(1)} %copy-done.3), kind=kOutput, calls=%fused_computation.163 | convolution fusion | flops 201355264 | bytes 3145728 | tf_op jit(solution)/shard_map/xyzc,kz->xykc/dot_general | solution.py:17
  52.5 11.0 %fusion.35 = f32[32,8,32,16]{2,0,3,1:T(8,128)} fusion(f32[32,8,64,16]{2,0,3,1:T(8,128)S(1)} %fusion.95, s32[64]{0:T(128)S(1)} %iota_add_fusion.1, s32[32]{0:T(128)S(1)} %pad_add_fusion), kind=kOutput, calls=%fused_computation.61 | convolution fusion | flops 100954112 | bytes 1573248 | tf_op jit(solution)/shard_map/xykc,qy->xqkc/dot_general | solution.py:17
  63.5 11.0 %add_bitcast_fusion.3 = f32[8,32,32,16]{2,1,3,0:T(8,128)} fusion(f32[32,8,32,16]{2,0,3,1:T(8,128)S(1)} %fusion.37, f32[32,8,64,16]{2,0,3,1:T(8,128)S(1)} %copy-done.4, s32[64]{0:T(128)S(1)} %iota_add_fusion.1, s32[32]{0:T(128)S(1)} %pad_add_fusion), kind=kOutput, calls=%fused_computation.82 | convolution fusion | flops 100823040 | bytes 2097536 | tf_op jit(solution)/shard_map/xykc,qy->xqkc/dot_general | solution.py:17
  80.2 12.6 %subtract_bitcast_fusion.3 = f32[8,32,32,16]{2,1,3,0:T(8,128)} fusion(f32[32,8,32,16]{2,0,3,1:T(8,128)} %fusion.35, f32[32,8,64,16]{2,0,3,1:T(8,128)S(1)} %copy-done.5, s32[64]{0:T(128)S(1)} %iota_add_fusion.1, s32[32]{0:T(128)S(1)} %pad_add_fusion), kind=kOutput, calls=%fused_computation.81 | convolution fusion | flops 100823040 | bytes 2097536 | tf_op jit(solution)/shard_map/xykc,qy->xqkc/dot_general | solution.py:17
  109.1 90.7 %reduce-scatter.11.cloned.1.call-done = f32[4,2,32,512]{3,2,1,0:T(8,128)} async-done(((f32[32,2,32,512]{3,2,1,0:T(8,128)}), f32[4,2,32,512]{3,2,1,0:T(8,128)}) %reduce-scatter.11.cloned.1.call-update) | async-done | bytes 524304 | tf_op jit(solution)/shard_map/reduce_scatter | solution.py:91
  210.1 19.2 %reshape_squeeze.6 = f32[4,2,16,32,16,16]{5,4,3,2,1,0:T(8,128)} reshape(f32[1,4,2,16,8192]{4,3,2,1,0:T(8,128)} %get-tuple-element.6) | data formatting | bytes 8388608 | tf_op jit(solution)/shard_map/reshape;squeeze | solution.py:100
  231.6 18.6 %fusion.1 = f32[4,16,32,1,16]{4,3,2,1,0:T(1,128)} fusion(f32[4,16,32,16,1]{3,4,2,1,0:T(1,128)S(1)} %bitcast.331, f32[4,2,16,32,16,16]{5,4,3,2,1,0:T(8,128)} %reshape_squeeze.6), kind=kOutput, calls=%fused_computation.5 | convolution fusion | flops 6291456 | bytes 17039360 | tf_op jit(solution)/shard_map/pqkc,pqkco->pqko/dot_general | solution.py:17
  250.1 17.0 %fusion.2 = f32[4,16,32,1,16]{4,3,2,1,0:T(1,128)S(1)} fusion(f32[4,16,32,16,1]{3,4,2,1,0:T(1,128)S(1)} %bitcast.332, f32[4,2,16,32,16,16]{5,4,3,2,1,0:T(8,128)} %reshape_squeeze.6), kind=kOutput, calls=%fused_computation.6 | convolution fusion | flops 6291456 | bytes 17039360 | tf_op jit(solution)/shard_map/pqkc,pqkco->pqko/dot_general | solution.py:17
  267.1 15.6 %fusion.3 = f32[4,16,32,1,16]{4,3,2,1,0:T(1,128)} fusion(f32[4,16,32,16,1]{3,4,2,1,0:T(1,128)S(1)} %bitcast.327, f32[4,2,16,32,16,16]{5,4,3,2,1,0:T(8,128)S(1)} %copy-done), kind=kOutput, calls=%fused_computation.7 | convolution fusion | flops 6291456 | bytes 17956864 | tf_op jit(solution)/shard_map/pqkc,pqkco->pqko/dot_general | solution.py:17
  282.7 14.9 %fusion = f32[4,16,32,1,16]{4,3,2,1,0:T(1,128)S(1)} fusion(f32[4,16,32,16,1]{3,4,2,1,0:T(1,128)S(1)} %bitcast.328, f32[4,2,16,32,16,16]{5,4,3,2,1,0:T(8,128)S(1)} %copy-done), kind=kOutput, calls=%fused_computation.4 | convolution fusion | flops 6291456 | bytes 17956864 | tf_op jit(solution)/shard_map/pqkc,pqkco->pqko/dot_general | solution.py:17
  305.7 49.2 %all-gather.5.cloned.1.call-done = f32[32,2,16,512]{3,2,1,0:T(8,128)} async-done(((f32[4,2,16,512]{3,2,1,0:T(8,128)}), f32[32,2,16,512]{3,2,1,0:T(8,128)}) %all-gather.5.cloned.1.call-update) | async-done | bytes 2097168 | tf_op jit(solution)/shard_map/all_gather | solution.py:109
  386.6 14.0 %fusion.9 = f32[8,64,64,16]{1,2,3,0:T(8,128)S(1)} fusion(f32[8,64,64,16]{1,3,2,0:T(8,128)S(1)} %copy-done.9, f32[64,8,64,16]{2,0,3,1:T(8,128)S(1)} %fusion.47, f32[8,64,32,16]{1,3,2,0:T(8,128)S(1)} %bitcast.350, f32[16]{0:T(128)S(1)} %get-tuple-element.20, f32[32]{0:T(128)S(1)} %fusion.205), kind=kOutput, calls=%fused_computation.15 | convolution fusion | flops 236484608 | bytes 7340224 | tf_op jit(solution)/shard_map/xyko,kz->xyzo/dot_general | solution.py:17
  414.9 11.0 %fusion.27 = f32[32,8,32,16]{2,0,3,1:T(8,128)} fusion(f32[32,8,64,16]{2,0,3,1:T(8,128)S(1)} %fusion.93, s32[64]{0:T(128)S(1)} %iota_add_fusion.1, s32[32]{0:T(128)S(1)} %pad_add_fusion), kind=kOutput, calls=%fused_computation.53 | convolution fusion | flops 100954112 | bytes 1573248 | tf_op jit(solution)/shard_map/xykc,qy->xqkc/dot_general | solution.py:17
  425.8 11.3 %add_bitcast_fusion.1 = f32[8,32,32,16]{2,1,3,0:T(8,128)} fusion(f32[32,8,32,16]{2,0,3,1:T(8,128)S(1)} %fusion.29, f32[32,8,64,16]{2,0,3,1:T(8,128)S(1)} %fusion.105, s32[64]{0:T(128)S(1)} %iota_add_fusion.1, s32[32]{0:T(128)S(1)} %pad_add_fusion), kind=kOutput, calls=%fused_computation.78 | convolution fusion | flops 100823040 | bytes 2097536 | tf_op jit(solution)/shard_map/xykc,qy->xqkc/dot_general | solution.py:17
  445.8 12.6 %subtract_bitcast_fusion.1 = f32[8,32,32,16]{2,1,3,0:T(8,128)} fusion(f32[32,8,32,16]{2,0,3,1:T(8,128)} %fusion.27, f32[32,8,64,16]{2,0,3,1:T(8,128)S(1)} %fusion.105, s32[64]{0:T(128)S(1)} %iota_add_fusion.1, s32[32]{0:T(128)S(1)} %pad_add_fusion), kind=kOutput, calls=%fused_computation.77 | convolution fusion | flops 100823040 | bytes 2097536 | tf_op jit(solution)/shard_map/xykc,qy->xqkc/dot_general | solution.py:17
  475.3 88.7 %reduce-scatter.13.cloned.1.call-done = f32[4,2,32,512]{3,2,1,0:T(8,128)} async-done(((f32[32,2,32,512]{3,2,1,0:T(8,128)}), f32[4,2,32,512]{3,2,1,0:T(8,128)}) %reduce-scatter.13.cloned.1.call-update) | async-done | bytes 524304 | tf_op jit(solution)/shard_map/reduce_scatter | solution.py:91
  566.7 19.2 %reshape_squeeze.7 = f32[4,2,16,32,16,16]{5,4,3,2,1,0:T(8,128)} reshape(f32[1,4,2,16,8192]{4,3,2,1,0:T(8,128)} %get-tuple-element.5) | data formatting | bytes 8388608 | tf_op jit(solution)/shard_map/reshape;squeeze | solution.py:100
  588.1 17.8 %fusion.7 = f32[4,16,32,1,16]{4,3,2,1,0:T(1,128)} fusion(f32[4,16,32,16,1]{3,4,2,1,0:T(1,128)S(1)} %bitcast.333, f32[4,2,16,32,16,16]{5,4,3,2,1,0:T(8,128)} %reshape_squeeze.7), kind=kOutput, calls=%fused_computation.11 | convolution fusion | flops 6291456 | bytes 17039360 | tf_op jit(solution)/shard_map/pqkc,pqkco->pqko/dot_general | solution.py:17
  605.9 17.0 %fusion.4 = f32[4,16,32,1,16]{4,3,2,1,0:T(1,128)S(1)} fusion(f32[4,16,32,16,1]{3,4,2,1,0:T(1,128)S(1)} %bitcast.334, f32[4,2,16,32,16,16]{5,4,3,2,1,0:T(8,128)} %reshape_squeeze.7), kind=kOutput, calls=%fused_computation.8 | convolution fusion | flops 6291456 | bytes 17039360 | tf_op jit(solution)/shard_map/pqkc,pqkco->pqko/dot_general | solution.py:17
  622.9 15.6 %fusion.5 = f32[4,16,32,1,16]{4,3,2,1,0:T(1,128)} fusion(f32[4,16,32,16,1]{3,4,2,1,0:T(1,128)S(1)} %bitcast.329, f32[4,2,16,32,16,16]{5,4,3,2,1,0:T(8,128)S(1)} %copy-done.1), kind=kOutput, calls=%fused_computation.9 | convolution fusion | flops 6291456 | bytes 17956864 | tf_op jit(solution)/shard_map/pqkc,pqkco->pqko/dot_general | solution.py:17
  638.4 14.9 %fusion.6 = f32[4,16,32,1,16]{4,3,2,1,0:T(1,128)S(1)} fusion(f32[4,16,32,16,1]{3,4,2,1,0:T(1,128)S(1)} %bitcast.330, f32[4,2,16,32,16,16]{5,4,3,2,1,0:T(8,128)S(1)} %copy-done.1), kind=kOutput, calls=%fused_computation.10 | convolution fusion | flops 6291456 | bytes 17956864 | tf_op jit(solution)/shard_map/pqkc,pqkco->pqko/dot_general | solution.py:17
  661.7 49.0 %all-gather.9.cloned.1.call-done = f32[32,2,16,512]{3,2,1,0:T(8,128)} async-done(((f32[4,2,16,512]{3,2,1,0:T(8,128)}), f32[32,2,16,512]{3,2,1,0:T(8,128)}) %all-gather.9.cloned.1.call-update) | async-done | bytes 2097168 | tf_op jit(solution)/shard_map/all_gather | solution.py:109
  753.7 13.5 %fusion.11 = f32[8,64,64,16]{1,2,3,0:T(8,128)S(1)} fusion(f32[8,64,64,16]{1,2,3,0:T(8,128)S(1)} %copy-done.10, f32[64,8,64,16]{2,0,3,1:T(8,128)S(1)} %fusion.44, f32[8,64,32,16]{1,3,2,0:T(8,128)S(1)} %bitcast.349, f32[16]{0:T(128)S(1)} %get-tuple-element.19, f32[32]{0:T(128)S(1)} %fusion.205), kind=kOutput, calls=%fused_computation.17 | convolution fusion | flops 236484608 | bytes 7340224 | tf_op jit(solution)/shard_map/xyko,kz->xyzo/dot_general | solution.py:17
  (142 shorter events, 197.2 us)
Async XLA Ops:
  6.5 193.3 %reduce-scatter.11.cloned.1.call-start = ((), (), s32[]{:S(2)}) async-start(), calls=%async_computation.4 | async-start | bytes 4718592 | tf_op jit(solution)/shard_map/reduce_scatter | solution.py:91
  15.9 13.8 %copy-start.3 = (f32[8,64,64,16]{2,1,3,0:T(8,128)S(1)}, f32[8,64,64,16]{2,1,3,0:T(8,128)}, u32[]{:S(2)}) copy-start(f32[8,64,64,16]{2,1,3,0:T(8,128)} %copy.75) | copy-start | bytes 6291460
  42.7 20.8 %copy-start.4 = (f32[32,8,64,16]{2,0,3,1:T(8,128)S(1)}, f32[32,8,64,16]{2,0,3,1:T(8,128)}, u32[]{:S(2)}) copy-start(f32[32,8,64,16]{2,0,3,1:T(8,128)} %fusion.107) | copy-start | bytes 3145732
  74.5 5.7 copy-start.5
  109.1 120.2 %reduce-scatter.15.cloned.1.call-start = ((), (), s32[]{:S(2)}) async-start(), calls=%async_computation.10 | async-start | bytes 786432
  202.4 152.5 %all-gather.5.cloned.1.call-start = ((), (), s32[]{:S(2)}) async-start(), calls=%async_computation.5 | async-start | bytes 2359296 | tf_op jit(solution)/shard_map/all_gather | solution.py:109
  231.5 35.6 %copy-start = (f32[4,2,16,32,16,16]{5,4,3,2,1,0:T(8,128)S(1)}, f32[4,2,16,32,16,16]{5,4,3,2,1,0:T(8,128)}, u32[]{:S(2)}) copy-start(f32[4,2,16,32,16,16]{5,4,3,2,1,0:T(8,128)} %reshape_squeeze.6) | copy-start | bytes 12582916
  282.7 14.9 %copy-start.7 = (f32[4,16,32,1,16]{4,3,2,1,0:T(1,128)S(1)}, f32[4,16,32,1,16]{4,3,2,1,0:T(1,128)}, u32[]{:S(2)}) copy-start(f32[4,16,32,1,16]{4,3,2,1,0:T(1,128)} %fusion.1) | copy-start | bytes 393220
  305.7 65.0 %all-gather.7.cloned.1.call-start = ((), (), s32[]{:S(2)}) async-start(), calls=%async_computation.6 | async-start | bytes 1572864 | tf_op jit(solution)/shard_map/all_gather | solution.py:118
  356.7 6.0 copy-start.14
  356.7 6.0 copy-start.13
  362.5 201.6 %reduce-scatter.13.cloned.1.call-start = ((), (), s32[]{:S(2)}) async-start(), calls=%async_computation.7 | async-start | bytes 4718592 | tf_op jit(solution)/shard_map/reduce_scatter | solution.py:91
  382.3 4.3 copy-start.9
  382.3 4.3 copy-start.12
  400.7 4.4 copy-start.2
  458.3 7.8 %copy-start.6 = (f32[32,32,512]{2,0,1:T(8,128)S(1)}, f32[32,32,512]{2,0,1:T(8,128)}, u32[]{:S(2)}) copy-start(f32[32,32,512]{2,0,1:T(8,128)} %fusion.179) | copy-start | bytes 6291460
  475.3 110.6 %reduce-scatter.17.cloned.1.call-start = ((), (), s32[]{:S(2)}) async-start(), calls=%async_computation.11 | async-start | bytes 786432
  566.6 144.1 %all-gather.9.cloned.1.call-start = ((), (), s32[]{:S(2)}) async-start(), calls=%async_computation.8 | async-start | bytes 2359296 | tf_op jit(solution)/shard_map/all_gather | solution.py:109
  588.1 34.8 %copy-start.1 = (f32[4,2,16,32,16,16]{5,4,3,2,1,0:T(8,128)S(1)}, f32[4,2,16,32,16,16]{5,4,3,2,1,0:T(8,128)}, u32[]{:S(2)}) copy-start(f32[4,2,16,32,16,16]{5,4,3,2,1,0:T(8,128)} %reshape_squeeze.7) | copy-start | bytes 12582916
  638.4 15.0 %copy-start.8 = (f32[4,16,32,1,16]{4,3,2,1,0:T(1,128)S(1)}, f32[4,16,32,1,16]{4,3,2,1,0:T(1,128)}, u32[]{:S(2)}) copy-start(f32[4,16,32,1,16]{4,3,2,1,0:T(1,128)} %fusion.7) | copy-start | bytes 393220
  661.4 76.5 %all-gather.11.cloned.1.call-start = ((), (), s32[]{:S(2)}) async-start(), calls=%async_computation.9 | async-start | bytes 1572864 | tf_op jit(solution)/shard_map/all_gather | solution.py:118
  749.6 4.1 copy-start.10
  749.6 4.1 copy-start.11
Sparse Core Ops, SparseCore 0:
  109.2 90.5 reduce-scatter.10
  202.5 7.6 reduce-scatter.14
  305.8 49.0 all-gather.4
  362.6 7.5 all-gather.6
  475.4 88.5 reduce-scatter.12
  566.7 7.7 reduce-scatter.16
  661.6 49.0 all-gather.8
  718.4 7.5 all-gather.10
where the time goes:
time: 787 us; the launch traced here: 782 us
  matrix products  345 us (44%)
  waiting for transfers between devices  278 us (35%)
  local copies, waits for them, and re-layouts  134 us (17%)
  between operations  14.4 us (2%)
  other arithmetic  10.5 us (1%)
    dot_general x50, matrix products, contract(): return jnp.einsum(form, left, right, precision=lax.Precision.HIGHEST)  345 us
    reduce_scatter x2, waiting for transfers between devices, shards(): lax.psum_scatter(term_first(jnp.int32(0), lax.axis_size('gx') * owned_x),...  179 us
    all_gather x2, waiting for transfers between devices, shards(): add_piece = lax.all_gather(mixed, 'gx', axis=0, tiled=True)  98.2 us
    another operation x2, local copies, waits for them, and re-layouts, shards(): tensor = weights.reshape(owned_x, 2, kept_y, MZ, C, C)  38.4 us
  transfers between devices with their start and end apart: 8, of which 4 were waited for; matrix products, arithmetic and copies ran while one was open for 9% of the time, Pallas kernels for 0%

commit v1 on v0

v1 whole, which is shorter than its diff:
```python
import functools
import math

import jax
import jax.numpy as jnp
import ml_dtypes
import numpy as np
from jax import lax
from jax.experimental import pallas as pl
from jax.experimental.pallas import tpu as pltpu
from jax.sharding import PartitionSpec as P

C = 16
MX = 32
MY = 32
MZ = 32
NZ = 64
LAYERS = 2
WIDTH = MZ * C
LANES = NZ * C
CHUNKS = 2
CW = WIDTH // CHUNKS
BLOCKS = CW // 128
MESH = pl.DeviceIdType.MESH


def signed_modes(count):
    half = count // 2
    return np.concatenate([np.arange(half), np.arange(half) - half])


def waves(frequencies, positions, length):
    angle = 2.0 * math.pi * ((frequencies[:, None] * positions[None, :]) % length) / length
    return np.cos(angle), np.sin(angle)


def pair(matrix):
    high = matrix.astype(np.float32).astype(ml_dtypes.bfloat16)
    low = (matrix - high.astype(np.float64)).astype(np.float32).astype(ml_dtypes.bfloat16)
    return np.stack([high, low])


def complex_rows(cosine, sine, sign):
    return np.stack([np.stack([cosine, -sign * sine], -1), np.stack([sign * sine, cosine], -1)], -2)


@functools.lru_cache(None)
def tables(n, pair_size, cells_x, cells_y):
    span_x, span_y = cells_x * n, cells_y * pair_size
    qs = MY // pair_size
    qn, pn = qs // n, MX // n
    eye = np.eye
    cosine, sine = waves(np.arange(MZ), np.arange(NZ), NZ)
    channels = eye(C)
    z_forward = np.einsum("pkz,cd->zcpkd", np.stack([cosine, -sine]), channels).reshape(LANES, 2 * WIDTH)
    scale = np.where(np.arange(MZ) == 0, 1.0, 2.0)[:, None] / (span_x * span_y * NZ)
    z_backward = np.einsum("pkz,cd->pkczd", np.stack([cosine * scale, -sine * scale]), channels).reshape(
        2 * WIDTH, LANES
    )
    y_forward, y_backward = [], []
    for g in range(pair_size):
        cosine, sine = waves(signed_modes(MY), g * cells_y + np.arange(cells_y), span_y)
        forward = complex_rows(cosine, sine, -1).reshape(pair_size, n, qn, cells_y, 2, 2)
        y_forward.append(
            pair(
                np.einsum("hdqyab,xw->hdxqabwy", forward, eye(cells_x)).reshape(
                    pair_size * n * cells_x * qn * 2, 2 * cells_x * cells_y
                )
            )
        )
        backward = complex_rows(cosine, sine, 1).reshape(pair_size, n, qn, cells_y, 2, 2)
        y_backward.append(
            pair(
                np.einsum("hdqyab,xw->awyhdxqb", backward, eye(cells_x)).reshape(
                    2 * cells_x * cells_y, pair_size * n * cells_x * qn * 2
                )
            )
        )
    cosine, sine = waves(signed_modes(MX), np.arange(span_x), span_x)
    rows = pn * qn * 2
    padded = max(8, rows)
    forward = complex_rows(cosine, sine, -1).reshape(n, pn, n, cells_x, 2, 2)
    x_forward = np.einsum("dpsxab,qr->dpqasxrb", forward, eye(qn)).reshape(n, rows, -1)
    x_forward = np.pad(x_forward, ((0, 0), (0, padded - rows), (0, 0))).reshape(n * padded, -1)
    backward = complex_rows(cosine, sine, 1).reshape(n, pn, n, cells_x, 2, 2)
    x_backward = np.einsum("dpsxab,qr->sxqadprb", backward, eye(qn)).reshape(-1, n, rows)
    x_backward = np.pad(x_backward, ((0, 0), (0, 0), (0, padded - rows))).reshape(-1, n * padded)
    order = np.zeros((pn, 2, n, qn, n, padded))
    for p in range(pn):
        for part in range(2):
            for s in range(n):
                for q in range(qn):
                    order[p, part, s, q, s, (p * qn + q) * 2 + part] = 1.0
    order = order.reshape(pn * 2 * qs, n * padded)
    spread = np.einsum("kl,cd,o->lckdo", eye(8), channels, np.ones(C)).reshape(128, 8, C * C)
    spread = np.concatenate([spread, spread]).transpose(1, 0, 2)
    gather = np.einsum("kl,c,op->kcolp", eye(8), np.ones(C), channels).reshape(8, C * C, 128)
    cast = lambda a: np.ascontiguousarray(a).astype(ml_dtypes.bfloat16)
    return dict(
        zf=pair(z_forward),
        zb=pair(z_backward),
        yf=np.stack(y_forward),
        yb=np.stack(y_backward),
        xf=pair(x_forward),
        xb=pair(x_backward),
        order=cast(order),
        back=cast(order.T),
        spread=cast(spread),
        gather=cast(gather),
    )


def split(value):
    high = value.astype(jnp.bfloat16)
    return high, (value - high.astype(jnp.float32)).astype(jnp.bfloat16)


def dot(left, right):
    return jnp.dot(left, right, preferred_element_type=jnp.float32)


def dot3(left, right):
    return dot(left[0], right[0]) + (dot(left[0], right[1]) + dot(left[1], right[0]))


def erf(x):
    x = jnp.clip(x, -4.0, 4.0)
    square = x * x
    top = jnp.float32(-2.72614225801306e-10)
    for c in (2.77068142495902e-08, -2.10102402082508e-06, -5.69250639462346e-05,
              -7.34990630326855e-04, -2.95459980854025e-03, -1.60960333262415e-02):
        top = top * square + c
    bottom = jnp.float32(-1.45660718464996e-05)
    for c in (-2.13374055278905e-04, -1.68282697438203e-03, -7.37332916720468e-03, -1.42647390514189e-02):
        bottom = bottom * square + c
    return x * top / bottom


def kernel(n, pn, cells, *refs):
    names = ("field", "spectral", "local", "bias", "zf", "yf", "xf", "order", "spread", "gather",
             "back", "xb", "yb", "zb")
    hbm = dict(zip(names, refs))
    out_hbm = refs[len(names)]
    (signal, weights, local, bias, zf, yf, xf, order, spread, gather, back, xb, yb, zb,
     s_high, s_low, z_high, z_low, b_high, b_low, p_high, p_low, total,
     send_y, recv_y, send_1, recv_1, send_2, recv_2, send_3, recv_3, send_4, recv_4, both,
     load_sem, pair_send, pair_recv, ring_send, ring_recv) = refs[len(names) + 1:]
    me = lax.axis_index("gx")
    core = lax.axis_index("gy")
    other = 1 - core
    rows_x = recv_1.shape[3]
    half = n * rows_x
    here = dict(field=signal, spectral=weights, local=local, bias=bias, zf=zf, yf=yf, xf=xf, order=order,
                spread=spread, gather=gather, back=back, xb=xb, yb=yb, zb=zb)
    loads = {}
    for at, name in enumerate(("field", "zf", "yf", "xf", "order", "spread", "spectral", "gather", "back", "xb",
                               "yb", "local", "bias", "zb")):
        source = hbm[name].at[core] if name in ("yf", "yb") else hbm[name]
        loads[name] = pltpu.make_async_copy(source, here[name], load_sem.at[at])
        loads[name].start()

    barrier = pltpu.get_barrier_semaphore()

    def greet(k, _):
        pl.semaphore_signal(barrier, inc=1, device_id={"gx": lax.rem(me + k, n)}, device_id_type=MESH)
        return 0

    lax.fori_loop(1, n, greet, 0)
    pl.semaphore_signal(barrier, inc=1, device_id={"gy": other}, device_id_type=MESH)
    pl.semaphore_wait(barrier, n)

    loads["field"].wait()

    def split_rows(i, _):
        at = pl.ds(pl.multiple_of(i * 64, 64), 64)
        s_high[at, :], s_low[at, :] = split(signal[at, :])
        return 0

    lax.fori_loop(0, cells // 64, split_rows, 0)
    for name in ("zf", "yf", "xf", "order", "spread", "spectral", "gather", "back", "xb", "yb", "local", "bias", "zb"):
        loads[name].wait()

    def ring_copy(stage, send, recv, layer, j, peer, slot, index):
        return pltpu.make_async_remote_copy(
            src_ref=send.at[layer, j, peer],
            dst_ref=recv.at[layer, j, slot],
            send_sem=ring_send.at[stage, layer, j, peer],
            recv_sem=ring_recv.at[stage, layer, j, slot],
            device_id={"gx": index},
            device_id_type=MESH,
        )

    def exchange(stage, send, recv, layer, j):
        def start(k, _):
            peer = lax.rem(me + k, n)
            ring_copy(stage, send, recv, layer, j, peer, me, peer).start()
            return 0

        lax.fori_loop(1, n, start, 0)
        recv[layer, j, me] = send[layer, j, me]

    def arrive(stage, send, recv, layer, j):
        def wait(k, _):
            peer = lax.rem(me + k, n)
            ring_copy(stage, send, recv, layer, j, peer, peer, peer).wait()
            return 0

        lax.fori_loop(1, n, wait, 0)

    def pair_copy(stage, send, recv, layer, j):
        return pltpu.make_async_remote_copy(
            src_ref=send,
            dst_ref=recv,
            send_sem=pair_send.at[stage, layer, j],
            recv_sem=pair_recv.at[stage, layer, j],
            device_id={"gy": other},
            device_id_type=MESH,
        )

    def run_layer(layer, _):
        def z_forward(t, _):
            lanes = pl.ds(pl.multiple_of(t * 256, 256), 256)
            value = dot3((s_high[...], s_low[...]), (zf[0, :, lanes], zf[1, :, lanes]))
            per = WIDTH // 256
            rows = pl.ds(pl.multiple_of((t // per) * cells, cells), cells)
            to = pl.ds(pl.multiple_of((t % per) * 256, 256), 256)
            z_high[rows, to], z_low[rows, to] = split(value)
            return 0

        def y_part(which, j):
            lanes = pl.ds(pl.multiple_of(j * CW, CW), CW)
            rows = pl.ds(pl.multiple_of(which * half, half), half)
            return dot3((yf[0, rows, :], yf[1, rows, :]), (z_high[:, lanes], z_low[:, lanes]))

        def y_forward(j, _):
            z_forward(j, 0)
            z_forward(j + CHUNKS, 0)
            send_y[layer, j] = y_part(other, j)
            pair_copy(0, send_y.at[layer, j], recv_y.at[layer, j], layer, j).start()
            send_1[layer, j] = y_part(core, j).reshape(n, rows_x, CW)
            return 0

        lax.fori_loop(0, CHUNKS, y_forward, 0)

        def x_send(j, _):
            pair_copy(0, send_y.at[layer, j], recv_y.at[layer, j], layer, j).wait()
            send_1[layer, j] = send_1[layer, j] + recv_y[layer, j].reshape(n, rows_x, CW)
            exchange(0, send_1, recv_1, layer, j)
            return 0

        lax.fori_loop(0, CHUNKS, x_send, 0)

        def x_forward(j, _):
            arrive(0, send_1, recv_1, layer, j)
            value = dot3((xf[0], xf[1]), split(recv_1[layer, j].reshape(half, CW)))
            send_2[layer, j] = value.reshape(send_2.shape[2:])
            exchange(1, send_2, recv_2, layer, j)
            return 0

        lax.fori_loop(0, CHUNKS, x_forward, 0)

        def mix(j, _):
            arrive(1, send_2, recv_2, layer, j)
            high, low = split(recv_2[layer, j].reshape(order.shape[1], CW))
            high = dot(order[...], high).astype(jnp.bfloat16)
            low = dot(order[...], low).astype(jnp.bfloat16)
            kept = order.shape[0]
            left = jnp.concatenate(
                [
                    jnp.concatenate([high[:, b * 128:(b + 1) * 128], low[:, b * 128:(b + 1) * 128]], 1)
                    for b in range(BLOCKS)
                ],
                0,
            )
            total[...] = jnp.zeros_like(total)

            def one_mode(k, _):
                modes = dot(left, spread[k])
                for b in range(BLOCKS):
                    lanes = pl.ds(pl.multiple_of(((j * BLOCKS + b) * 8 + k) * 256, 256), 256)
                    for p in range(pn):
                        at = b * kept + p * 32
                        real, imaginary = modes[at:at + 16], modes[at + 16:at + 32]
                        w_real = weights[layer, p, 0, :, lanes]
                        w_imaginary = weights[layer, p, 1, :, lanes]
                        p_high[at:at + 16, :], p_low[at:at + 16, :] = split(real * w_real - imaginary * w_imaginary)
                        p_high[at + 16:at + 32, :], p_low[at + 16:at + 32, :] = split(
                            real * w_imaginary + imaginary * w_real
                        )
                total[...] += dot(p_high[...], gather[k]) + dot(p_low[...], gather[k])
                return 0

            lax.fori_loop(0, 8, one_mode, 0)
            mixed = jnp.concatenate([total[b * kept:(b + 1) * kept, :] for b in range(BLOCKS)], 1)
            high, low = split(mixed)
            send_3[layer, j] = (dot(back[...], high) + dot(back[...], low)).reshape(send_3.shape[2:])
            exchange(2, send_3, recv_3, layer, j)
            return 0

        lax.fori_loop(0, CHUNKS, mix, 0)

        def x_backward(j, _):
            arrive(2, send_3, recv_3, layer, j)
            value = dot3((xb[0], xb[1]), split(recv_3[layer, j].reshape(order.shape[1], CW)))
            send_4[layer, j] = value.reshape(n, rows_x, CW)
            exchange(3, send_4, recv_4, layer, j)
            return 0

        lax.fori_loop(0, CHUNKS, x_backward, 0)

        def y_send(j, _):
            arrive(3, send_4, recv_4, layer, j)
            both[layer, j, core] = recv_4[layer, j].reshape(half, CW)
            pair_copy(1, both.at[layer, j, core], both.at[layer, j, core], layer, j).start()
            return 0

        lax.fori_loop(0, CHUNKS, y_send, 0)

        def y_backward(j, _):
            pair_copy(1, both.at[layer, j, core], both.at[layer, j, other], layer, j).wait()
            high, low = split(both[layer, j].reshape(2 * half, CW))
            for part in range(2):
                at = slice(part * cells, (part + 1) * cells)
                value = dot3((yb[0, at, :], yb[1, at, :]), (high, low))
                lanes = pl.ds(pl.multiple_of(part * WIDTH + j * CW, CW), CW)
                b_high[:, lanes], b_low[:, lanes] = split(value)
            return 0

        lax.fori_loop(0, CHUNKS, y_backward, 0)
        local_pair = split(local[layer])

        def z_backward(t, _):
            lanes = pl.ds(pl.multiple_of(t * 256, 256), 256)
            value = dot3((b_high[...], b_low[...]), (zb[0, :, lanes], zb[1, :, lanes]))
            value += dot3((s_high[:, lanes], s_low[:, lanes]), local_pair)
            value += bias[layer]
            value = 0.5 * value * (1.0 + erf(value * math.sqrt(0.5)))
            signal[:, lanes] = value
            s_high[:, lanes], s_low[:, lanes] = split(value)
            return 0

        lax.fori_loop(0, LANES // 256, z_backward, 0)
        return 0

    lax.fori_loop(0, LAYERS, run_layer, 0)
    store = pltpu.make_async_copy(signal, out_hbm, load_sem.at[0])
    store.start()
    store.wait()


def shards(field, spectral, mixing, bias):
    cells_x, cells_y = field.shape[:2]
    n, pair_size = lax.axis_size("gx"), lax.axis_size("gy")
    cells = cells_x * cells_y
    table = tables(n, pair_size, cells_x, cells_y)
    pn = spectral.shape[1]
    qs = spectral.shape[3]
    rows_x = cells_x * (qs // n) * 2
    rows_p = table["xf"].shape[1] // n
    local = jnp.tile(mixing, (1, 16, 16)) * jnp.asarray(np.kron(np.eye(16), np.ones((C, C))), jnp.float32)
    wide_bias = jnp.tile(bias, (1, 16))[:, None, :]
    operands = [field.reshape(cells, LANES), spectral, local, wide_bias] + [
        jnp.asarray(table[name])
        for name in ("zf", "yf", "xf", "order", "spread", "gather", "back", "xb", "yb", "zb")
    ]
    f32, bf16 = jnp.float32, jnp.bfloat16
    loaded = []
    for at, operand in enumerate(operands):
        shape = operand.shape[1:] if at in (5, 12) else operand.shape
        loaded.append(pltpu.VMEM(shape, operand.dtype))
    half = n * rows_x
    kept = pn * 2 * qs
    scratch = loaded + [
        pltpu.VMEM((cells, LANES), bf16),
        pltpu.VMEM((cells, LANES), bf16),
        pltpu.VMEM((2 * cells, WIDTH), bf16),
        pltpu.VMEM((2 * cells, WIDTH), bf16),
        pltpu.VMEM((cells, 2 * WIDTH), bf16),
        pltpu.VMEM((cells, 2 * WIDTH), bf16),
        pltpu.VMEM((BLOCKS * kept, 256), bf16),
        pltpu.VMEM((BLOCKS * kept, 256), bf16),
        pltpu.VMEM((BLOCKS * kept, 128), f32),
        pltpu.VMEM((LAYERS, CHUNKS, half, CW), f32),
        pltpu.VMEM((LAYERS, CHUNKS, half, CW), f32),
    ]
    for rows in (rows_x, rows_p, rows_p, rows_x):
        scratch += [pltpu.VMEM((LAYERS, CHUNKS, n, rows, CW), f32)] * 2
    scratch += [
        pltpu.VMEM((LAYERS, CHUNKS, 2, half, CW), f32),
        pltpu.SemaphoreType.DMA((len(operands),)),
        pltpu.SemaphoreType.DMA((2, LAYERS, CHUNKS)),
        pltpu.SemaphoreType.DMA((2, LAYERS, CHUNKS)),
        pltpu.SemaphoreType.DMA((4, LAYERS, CHUNKS, n)),
        pltpu.SemaphoreType.DMA((4, LAYERS, CHUNKS, n)),
    ]
    result = pl.pallas_call(
        functools.partial(kernel, n, pn, cells),
        out_shape=jax.ShapeDtypeStruct((cells, LANES), f32),
        in_specs=[pl.BlockSpec(memory_space=pl.ANY)] * len(operands),
        out_specs=pl.BlockSpec(memory_space=pl.ANY),
        scratch_shapes=scratch,
        compiler_params=pltpu.CompilerParams(
            collective_id=0, has_side_effects=True, vmem_limit_bytes=60 * 1024 * 1024
        ),
    )(*operands)
    return result.reshape(cells_x, cells_y, LANES)


def solution(mesh):
    placed = (P(("groups", "gx"), "gy", None), P(None, "gx", None, "gy", None), P(), P())
    return jax.shard_map(
        shards,
        mesh=mesh,
        in_specs=placed,
        out_specs=P(("groups", "gx"), "gy", None),
        check_vma=False,
    )
```

time: 787 us -> 139 us (0.18)
  matrix products: 345 us -> 0 us
  waiting for transfers between devices: 278 us -> 0 us
  Pallas kernels: 0 us -> 127 us
  local copies, waits for them, and re-layouts: 134 us -> 10.5 us
  between operations: 14.4 us -> 0.03 us
  other arithmetic: 10.5 us -> 0.84 us
    dot_general x50 -> x0, matrix products: 345 us -> none  [contract(): return jnp.einsum(form, left, right, precision=lax.Precision.HIGHEST)]
    reduce_scatter x2 -> x0, waiting for transfers between devices: 179 us -> none  [shards(): lax.psum_scatter(term_first(jnp.int32(0), lax.axis_size('gx') * owned_x),...]
    pallas_call x0 -> x1, Pallas kernels: none -> 127 us  [shards(): pl.pallas_call(functools.partial(kernel, n, pn, cells), out_shape=jax.Sha...]
    all_gather x4 -> x0, waiting for transfers between devices: 98.2 us -> none  [the longest x2 98.2 us: shards(): add_piece = lax.all_gather(mixed, 'gx', axis=0, tiled=True)]
    another operation x10 -> x4, local copies, waits for them, and re-layouts: 56 us -> 7.33 us  [the longest x2 6.65 us: shards(): jnp.tile(mixing, (1, 16, 16))]
    slice x5 -> x0, local copies, waits for them, and re-layouts: 11.7 us -> none  [the longest x1 7.72 us: shards(): weights = spectral[layer]]
    reshape x4 -> x0, local copies, waits for them, and re-layouts: 10.7 us -> none  [the longest x1 5.55 us: shards(): signal = field.reshape(cells_x, cells_y, NZ, C)]
    add x5 -> x0, local copies, waits for them, and re-layouts: 10.3 us -> none  [the longest x2 6.43 us: shards(): contract('xykc,qy->xqkc', z_real, y_cosine)]
  transfers between devices with their start and end apart: 8 -> 0, of which waited for: 4 -> 0; matrix products, arithmetic and copies ran while one was open for 9% -> 0% of each run, Pallas kernels for 0% -> 0%
where the time goes in v1:
time: 139 us; the launch traced here: 138 us
  Pallas kernels  127 us (91%)
  local copies, waits for them, and re-layouts  10.5 us (8%)
    pallas_call x1, Pallas kernels, shards(): pl.pallas_call(functools.partial(kernel, n, pn, cells), out_shape=jax.Sha...  127 us
    another operation x2, local copies, waits for them, and re-layouts, shards(): jnp.tile(mixing, (1, 16, 16))  6.65 us
    unnamed x5, local copies, waits for them, and re-layouts  3.17 us

profile of v1, /device:TPU:0, one launch (start us, length us, event | category | flops | bytes accessed | tf_op | source)
XLA Modules:
  0.0 138.4 jit_solution(8592000913173153647)
XLA Ops:
  0.0 0.0 copy-start
  0.0 0.0 copy-start.1
  0.0 3.2 %tile.8 = f32[2,16,16,16,16]{4,3,2,1,0:T(8,128)} broadcast(f32[2,16,16]{2,1,0:T(8,128)} %param.17), dimensions={0,2,4} | broadcast | bytes 526336 | tf_op jit(solution)/shard_map/tile | solution.py:360
  3.2 3.5 %tile.18 = f32[2,256,256]{2,1,0:T(8,128)S(1)} reshape(f32[2,16,16,16,16]{4,3,2,1,0:T(8,128)} %tile.8) | data formatting | bytes 1048576 | tf_op jit(solution)/shard_map/tile | solution.py:360
  6.7 0.0 copy-done
  6.7 0.8 broadcast_multiply_fusion.refs_2_
  7.5 0.0 copy-done.1
  7.5 0.7 tile.20.refs_3_
  8.2 127.1 %shard_map.145 = f32[512,1024]{1,0:T(8,128)} custom-call(f32[512,1024]{1,0:T(8,128)} %bitcast.5, f32[2,4,2,16,8192]{4,3,2,1,0:T(8,128)} %refs_1_.1, f32[2,256,256]{2,1,0:T(8,128)} %broadcast_multiply_fusion.refs_2_, f32[2,1,256]{2,1,0:T(1,128)} %tile.20.refs_3_, bf16[2,1024,1024]{2,1,0:T(8,128)(2,1)} %constant.23.clone.refs_4_, ...), custom_call_target="tpu_custom_call" | custom-call | tf_op jit(solution)/shard_map/pallas_call | solution.py:396
  135.3 3.2 %copy.17 = f32[8,64,1024]{2,1,0:T(8,128)} copy(f32[8,64,1024]{2,1,0:T(8,128)} %bitcast.4) | data formatting | bytes 4194304
  (1 shorter events, 0.0 us)
Async XLA Ops:
  0.0 6.7 %copy-start = (f32[256,256]{1,0:T(8,128)S(1)}, f32[256,256]{1,0:T(8,128)}, u32[]{:S(2)}) copy-start(f32[256,256]{1,0:T(8,128)} %constant.22.clone) | copy-start | bytes 786436
  0.0 7.5 %copy-start.1 = (f32[2,16]{1,0:T(2,128)S(1)}, f32[2,16]{1,0:T(2,128)}, u32[]{:S(2)}) copy-start(f32[2,16]{1,0:T(2,128)} %param.18) | copy-start | bytes 388

commit v2 on v1

v2 whole, which is shorter than its diff:
```python
import functools
import math

import jax
import jax.numpy as jnp
import ml_dtypes
import numpy as np
from jax import lax
from jax.experimental import pallas as pl
from jax.experimental.pallas import tpu as pltpu
from jax.sharding import PartitionSpec as P

C = 16
MX = 32
MY = 32
MZ = 32
NZ = 64
LAYERS = 2
WIDTH = MZ * C
LANES = NZ * C
CHUNKS = 2
CW = WIDTH // CHUNKS
BLOCKS = CW // 128
UNROLL = 4
HALVES = 2
MESH = pl.DeviceIdType.MESH


def signed_modes(count):
    half = count // 2
    return np.concatenate([np.arange(half), np.arange(half) - half])


def waves(frequencies, positions, length):
    angle = 2.0 * math.pi * ((frequencies[:, None] * positions[None, :]) % length) / length
    return np.cos(angle), np.sin(angle)


def pair(matrix):
    high = matrix.astype(np.float32).astype(ml_dtypes.bfloat16)
    low = (matrix - high.astype(np.float64)).astype(np.float32).astype(ml_dtypes.bfloat16)
    return np.stack([high, low])


def complex_rows(cosine, sine, sign):
    return np.stack([np.stack([cosine, -sign * sine], -1), np.stack([sign * sine, cosine], -1)], -2)


@functools.lru_cache(None)
def tables(n, pair_size, cells_x, cells_y):
    span_x, span_y = cells_x * n, cells_y * pair_size
    qs = MY // pair_size
    qn, pn = qs // n, MX // n
    eye = np.eye
    part_x = cells_x // HALVES
    cosine, sine = waves(np.arange(MZ), np.arange(NZ), NZ)
    channels = eye(C)
    z_forward = np.einsum("pkz,cd->zcpkd", np.stack([cosine, -sine]), channels).reshape(LANES, 2 * WIDTH)
    scale = np.where(np.arange(MZ) == 0, 1.0, 2.0)[:, None] / (span_x * span_y * NZ)
    z_backward = np.einsum("pkz,cd->pkczd", np.stack([cosine * scale, -sine * scale]), channels).reshape(
        2 * WIDTH, LANES
    )
    y_forward, y_backward = [], []
    for g in range(pair_size):
        cosine, sine = waves(signed_modes(MY), g * cells_y + np.arange(cells_y), span_y)
        forward = complex_rows(cosine, sine, -1).reshape(pair_size, n, qn, cells_y, 2, 2)
        y_forward.append(
            pair(
                np.einsum("hdqyab,xw->hdxqabwy", forward, eye(part_x)).reshape(
                    pair_size * n * part_x * qn * 2, 2 * part_x * cells_y
                )
            )
        )
        backward = complex_rows(cosine, sine, 1).reshape(pair_size, n, qn, cells_y, 2, 2)
        y_backward.append(
            pair(
                np.einsum("hdqyab,xw->awyhdxqb", backward, eye(part_x)).reshape(
                    2 * part_x * cells_y, pair_size * n * part_x * qn * 2
                )
            )
        )
    cosine, sine = waves(signed_modes(MX), np.arange(span_x), span_x)
    rows = pn * qn * 2
    padded = max(8, rows)
    forward = complex_rows(cosine, sine, -1).reshape(n, pn, n, HALVES, part_x, 2, 2)
    x_forward = np.einsum("dpshxab,qr->dpqahsxrb", forward, eye(qn)).reshape(n, rows, -1)
    x_forward = np.pad(x_forward, ((0, 0), (0, padded - rows), (0, 0))).reshape(n * padded, -1)
    backward = complex_rows(cosine, sine, 1).reshape(n, pn, n, HALVES, part_x, 2, 2)
    x_backward = np.einsum("dpshxab,qr->hsxqadprb", backward, eye(qn)).reshape(-1, n, rows)
    x_backward = np.pad(x_backward, ((0, 0), (0, 0), (0, padded - rows))).reshape(-1, n * padded)
    order = np.zeros((pn, 2, n, qn, n, padded))
    for p in range(pn):
        for part in range(2):
            for s in range(n):
                for q in range(qn):
                    order[p, part, s, q, s, (p * qn + q) * 2 + part] = 1.0
    order = order.reshape(pn * 2 * qs, n * padded)
    spread = np.einsum("kl,cd,o->lckdo", eye(8), channels, np.ones(C)).reshape(128, 8, C * C)
    spread = np.concatenate([spread, spread]).transpose(1, 0, 2)
    gather = np.einsum("kl,c,op->kcolp", eye(8), np.ones(8), channels).reshape(8, 128, 128)
    gather = np.concatenate([gather, gather], 1).reshape(8 * 256, 128)
    tile = np.kron(np.ones((16, 1)), channels)
    cast = lambda a: np.ascontiguousarray(a).astype(ml_dtypes.bfloat16)
    return dict(
        zf=pair(z_forward),
        zb=pair(z_backward),
        yf=np.stack(y_forward),
        yb=np.stack(y_backward),
        xf=pair(x_forward),
        xb=pair(x_backward),
        order=cast(order),
        back=cast(order.T),
        spread=cast(spread),
        gather=cast(gather),
        tile=cast(tile),
        across=cast(tile.T),
    )


def split(value):
    high = value.astype(jnp.bfloat16)
    return high, (value - high.astype(jnp.float32)).astype(jnp.bfloat16)


def dot(left, right):
    return jnp.dot(left, right, preferred_element_type=jnp.float32)


def dot3(left, right):
    return dot(left[0], right[0]) + (dot(left[0], right[1]) + dot(left[1], right[0]))


def erf(x):
    x = jnp.clip(x, -4.0, 4.0)
    square = x * x
    top = jnp.float32(-2.72614225801306e-10)
    for c in (2.77068142495902e-08, -2.10102402082508e-06, -5.69250639462346e-05,
              -7.34990630326855e-04, -2.95459980854025e-03, -1.60960333262415e-02):
        top = top * square + c
    bottom = jnp.float32(-1.45660718464996e-05)
    for c in (-2.13374055278905e-04, -1.68282697438203e-03, -7.37332916720468e-03, -1.42647390514189e-02):
        bottom = bottom * square + c
    return x * top / bottom


def kernel(n, pn, cells, *refs):
    names = ("field", "spectral", "mixing", "bias", "zf", "yf", "xf", "order", "spread", "gather",
             "back", "xb", "yb", "zb", "tile", "across")
    hbm = dict(zip(names, refs))
    out_hbm = refs[len(names)]
    (signal, weights, mixing, bias, zf, yf, xf, order, spread, gather, back, xb, yb, zb, tile, across,
     s_high, s_low, z_high, z_low, b_high, b_low, product, local_high, local_low, wide_bias,
     send_y, recv_y, send_1, recv_1, send_2, recv_2, send_3, recv_3, send_4, recv_4, both,
     load_sem, store_sem, pair_send, pair_recv, outer_send, outer_recv, inner_send, inner_recv) = refs[len(names) + 1:]
    me = lax.axis_index("gx")
    core = lax.axis_index("gy")
    other = 1 - core
    rows_x = recv_1.shape[4]
    quarter = n * rows_x
    part_cells = cells // HALVES
    here = dict(field=signal, spectral=weights, mixing=mixing, bias=bias, zf=zf, yf=yf, xf=xf, order=order,
                spread=spread, gather=gather, back=back, xb=xb, yb=yb, zb=zb, tile=tile, across=across)
    loads = {}
    for at, name in enumerate(("field", "zf", "yf", "xf", "order", "spread", "spectral", "gather", "back", "xb",
                               "yb", "mixing", "bias", "tile", "across", "zb")):
        source = hbm[name].at[core] if name in ("yf", "yb") else hbm[name]
        loads[name] = pltpu.make_async_copy(source, here[name], load_sem.at[at])
        loads[name].start()

    barrier = pltpu.get_barrier_semaphore()

    def greet(k, _):
        pl.semaphore_signal(barrier, inc=1, device_id={"gx": lax.rem(me + k, n)}, device_id_type=MESH)
        return 0

    lax.fori_loop(1, n, greet, 0)
    pl.semaphore_signal(barrier, inc=1, device_id={"gy": other}, device_id_type=MESH)

    def copy_to(send, recv, sems, peer, slot):
        return pltpu.make_async_remote_copy(
            src_ref=send.at[peer],
            dst_ref=recv.at[slot],
            send_sem=sems[0].at[peer],
            recv_sem=sems[1].at[slot],
            device_id={"gx": peer},
            device_id_type=MESH,
        )

    def exchange(send, recv, sems):
        def start(k, _):
            peer = lax.rem(me + k, n)
            copy_to(send, recv, sems, peer, me).start()
            return 0

        lax.fori_loop(1, n, start, 0)
        recv[me] = send[me]

    def arrive(send, recv, sems):
        def wait(k, _):
            peer = lax.rem(me + k, n)
            copy_to(send, recv, sems, peer, peer).wait()
            return 0

        lax.fori_loop(1, n, wait, 0)

    def outer(way, layer, j, h):
        sends, recvs = ((send_1, recv_1), (send_4, recv_4))[way]
        return (sends.at[layer, j, h], recvs.at[layer, j, h],
                (outer_send.at[way, layer, j, h], outer_recv.at[way, layer, j, h]))

    def inner(way, layer, j):
        sends, recvs = ((send_2, recv_2), (send_3, recv_3))[way]
        return (sends.at[layer, j], recvs.at[layer, j],
                (inner_send.at[way, layer, j], inner_recv.at[way, layer, j]))

    def pair_copy(way, layer, h, arriving=False):
        if way == 0:
            src, dst = send_y.at[layer, h, other], recv_y.at[layer, h]
        else:
            src, dst = both.at[layer, h, core], both.at[layer, h, other if arriving else core]
        return pltpu.make_async_remote_copy(
            src_ref=src,
            dst_ref=dst,
            send_sem=pair_send.at[way, layer, h],
            recv_sem=pair_recv.at[way, layer, h],
            device_id={"gy": other},
            device_id_type=MESH,
        )

    def z_forward(h):
        rows = pl.ds(h * part_cells, part_cells)

        def one(t, _):
            lanes = pl.ds(pl.multiple_of(t * 256, 256), 256)
            value = dot3((s_high[rows, :], s_low[rows, :]), (zf[0, :, lanes], zf[1, :, lanes]))
            per = WIDTH // 256
            to_rows = pl.ds(pl.multiple_of((t // per) * part_cells, part_cells), part_cells)
            to = pl.ds(pl.multiple_of((t % per) * 256, 256), 256)
            z_high[to_rows, to], z_low[to_rows, to] = split(value)
            return 0

        lax.fori_loop(0, 2 * WIDTH // 256, one, 0, unroll=UNROLL)

    def y_forward(layer, h):
        value = dot3((yf[0], yf[1]), (z_high[...], z_low[...]))
        send_y[layer, h] = value.reshape(2, quarter, WIDTH)
        pair_copy(0, layer, h).start()

    def x_send(layer, h):
        pair_copy(0, layer, h).wait()
        for j in range(CHUNKS):
            lanes = slice(j * CW, (j + 1) * CW)
            value = send_y[layer, h, core, :, lanes] + recv_y[layer, h, :, lanes]
            send_1[layer, j, h] = value.reshape(n, rows_x, CW)
            exchange(*outer(0, layer, j, h))

    def x_forward(layer, j):
        for h in range(HALVES):
            arrive(*outer(0, layer, j, h))
        value = dot3((xf[0], xf[1]), split(recv_1[layer, j].reshape(HALVES * quarter, CW)))
        send_2[layer, j] = value.reshape(send_2.shape[2:])
        exchange(*inner(0, layer, j))

    def mix(layer, j):
        arrive(*inner(0, layer, j))
        high, low = split(recv_2[layer, j].reshape(order.shape[1], CW))
        high = dot(order[...], high).astype(jnp.bfloat16)
        low = dot(order[...], low).astype(jnp.bfloat16)
        kept = order.shape[0]
        left = jnp.concatenate(
            [
                jnp.concatenate([high[:, b * 128:(b + 1) * 128], low[:, b * 128:(b + 1) * 128]], 1)
                for b in range(BLOCKS)
            ],
            0,
        )
        for k in range(8):
            modes = dot(left, spread[k])
            for b in range(BLOCKS):
                lanes = pl.ds(((j * BLOCKS + b) * 8 + k) * 256, 256)
                for p in range(pn):
                    at = b * kept + p * 32
                    real, imaginary = modes[at:at + 16], modes[at + 16:at + 32]
                    w_real = weights[layer, p, 0, :, lanes]
                    w_imaginary = weights[layer, p, 1, :, lanes]
                    for shift, term in (
                        (0, real * w_real - imaginary * w_imaginary),
                        (16, real * w_imaginary + imaginary * w_real),
                    ):
                        high, low = split(term[:, :128] + term[:, 128:])
                        product[at + shift:at + shift + 16, k * 256:k * 256 + 128] = high
                        product[at + shift:at + shift + 16, k * 256 + 128:k * 256 + 256] = low
        total = dot(product[...], gather[...])
        mixed = jnp.concatenate([total[b * kept:(b + 1) * kept, :] for b in range(BLOCKS)], 1)
        high, low = split(mixed)
        send_3[layer, j] = (dot(back[...], high) + dot(back[...], low)).reshape(send_3.shape[2:])
        exchange(*inner(1, layer, j))

    def x_backward(layer, j):
        arrive(*inner(1, layer, j))
        value = dot3((xb[0], xb[1]), split(recv_3[layer, j].reshape(order.shape[1], CW)))
        send_4[layer, j] = value.reshape(send_4.shape[2:])
        for h in range(HALVES):
            exchange(*outer(1, layer, j, h))

    def y_send(layer, h):
        for j in range(CHUNKS):
            arrive(*outer(1, layer, j, h))
            both[layer, h, core, :, j * CW:(j + 1) * CW] = recv_4[layer, j, h].reshape(quarter, CW)
        pair_copy(1, layer, h).start()

    def y_backward(layer, h):
        pair_copy(1, layer, h, arriving=True).wait()
        high, low = split(both[layer, h].reshape(2 * quarter, WIDTH))
        for part in range(2):
            at = slice(part * part_cells, (part + 1) * part_cells)
            lanes = slice(part * WIDTH, (part + 1) * WIDTH)
            b_high[:, lanes], b_low[:, lanes] = split(dot3((yb[0, at, :], yb[1, at, :]), (high, low)))

    def z_backward(layer, h):
        rows = pl.ds(h * part_cells, part_cells)
        local = (local_high[layer], local_low[layer])

        def one(t, _):
            lanes = pl.ds(pl.multiple_of(t * 256, 256), 256)
            value = dot3((b_high[...], b_low[...]), (zb[0, :, lanes], zb[1, :, lanes]))
            value += dot3((s_high[rows, lanes], s_low[rows, lanes]), local)
            value += wide_bias[layer]
            value = 0.5 * value * (1.0 + erf(value * math.sqrt(0.5)))
            signal[rows, lanes] = value
            s_high[rows, lanes], s_low[rows, lanes] = split(value)
            return 0

        lax.fori_loop(0, LANES // 256, one, 0, unroll=UNROLL)

    loads["field"].wait()

    def split_rows(i, _):
        at = pl.ds(pl.multiple_of(i * 64, 64), 64)
        s_high[at, :], s_low[at, :] = split(signal[at, :])
        return 0

    lax.fori_loop(0, cells // 64, split_rows, 0)
    loads["zf"].wait()
    z_forward(0)
    pl.semaphore_wait(barrier, n)
    loads["yf"].wait()
    y_forward(0, 0)
    z_forward(1)
    x_send(0, 0)
    y_forward(0, 1)
    for name in ("mixing", "bias", "tile", "across"):
        loads[name].wait()
    same = (lax.broadcasted_iota(jnp.int32, (256, 256), 0) // C
            == lax.broadcasted_iota(jnp.int32, (256, 256), 1) // C)
    for layer in range(LAYERS):
        for term, to in zip(split(mixing[layer]), (local_high, local_low)):
            wide = dot(dot(tile[...], term).astype(jnp.bfloat16), across[...])
            to[layer] = jnp.where(same, wide, 0.0).astype(jnp.bfloat16)
        high, rest = split(bias[layer:layer + 1, :])
        middle, low = split(bias[layer:layer + 1, :] - high.astype(jnp.float32))
        wide_bias[layer] = dot(high, across[...]) + (dot(middle, across[...]) + dot(low, across[...]))
    x_send(0, 1)
    for name in ("xf", "order", "spread", "spectral", "gather", "back", "xb", "yb", "zb"):
        loads[name].wait()

    def run_layer(layer, _):
        for stage in (x_forward, mix, x_backward):
            for j in range(CHUNKS):
                stage(layer, j)
        more = layer + 1 < LAYERS
        y_send(layer, 0)
        y_backward(layer, 0)
        z_backward(layer, 0)

        @pl.when(more)
        def _():
            z_forward(0)
            y_forward(layer + 1, 0)

        y_send(layer, 1)

        @pl.when(more)
        def _():
            x_send(layer + 1, 0)

        y_backward(layer, 1)
        z_backward(layer, 1)

        @pl.when(more)
        def _():
            z_forward(1)
            y_forward(layer + 1, 1)
            x_send(layer + 1, 1)

        return 0

    lax.fori_loop(0, LAYERS, run_layer, 0)
    store = pltpu.make_async_copy(signal, out_hbm, store_sem)
    store.start()
    store.wait()


def shards(field, spectral, mixing, bias):
    cells_x, cells_y = field.shape[:2]
    n, pair_size = lax.axis_size("gx"), lax.axis_size("gy")
    cells = cells_x * cells_y
    table = tables(n, pair_size, cells_x, cells_y)
    pn = spectral.shape[1]
    qs = spectral.shape[3]
    rows_x = cells_x // HALVES * (qs // n) * 2
    rows_p = table["xf"].shape[1] // n
    operands = [field.reshape(cells, LANES), spectral, mixing, bias] + [
        jnp.asarray(table[name])
        for name in ("zf", "yf", "xf", "order", "spread", "gather", "back", "xb", "yb", "zb", "tile", "across")
    ]
    f32, bf16 = jnp.float32, jnp.bfloat16
    scratch = []
    for at, operand in enumerate(operands):
        shape = operand.shape[1:] if at in (5, 12) else operand.shape
        scratch.append(pltpu.VMEM(shape, operand.dtype))
    quarter = n * rows_x
    kept = pn * 2 * qs
    part_cells = cells // HALVES
    scratch += [pltpu.VMEM((cells, LANES), bf16)] * 2
    scratch += [pltpu.VMEM((2 * part_cells, WIDTH), bf16)] * 2
    scratch += [pltpu.VMEM((part_cells, 2 * WIDTH), bf16)] * 2
    scratch += [
        pltpu.VMEM((BLOCKS * kept, 8 * 256), bf16),
        pltpu.VMEM((LAYERS, 256, 256), bf16),
        pltpu.VMEM((LAYERS, 256, 256), bf16),
        pltpu.VMEM((LAYERS, 1, 256), f32),
        pltpu.VMEM((LAYERS, HALVES, 2, quarter, WIDTH), f32),
        pltpu.VMEM((LAYERS, HALVES, quarter, WIDTH), f32),
    ]
    for shape in ((HALVES, n, rows_x), (n, rows_p), (n, rows_p), (HALVES, n, rows_x)):
        scratch += [pltpu.VMEM((LAYERS, CHUNKS) + shape + (CW,), f32)] * 2
    scratch += [
        pltpu.VMEM((LAYERS, HALVES, 2, quarter, WIDTH), f32),
        pltpu.SemaphoreType.DMA((len(operands),)),
        pltpu.SemaphoreType.DMA,
        pltpu.SemaphoreType.DMA((2, LAYERS, HALVES)),
        pltpu.SemaphoreType.DMA((2, LAYERS, HALVES)),
        pltpu.SemaphoreType.DMA((2, LAYERS, CHUNKS, HALVES, n)),
        pltpu.SemaphoreType.DMA((2, LAYERS, CHUNKS, HALVES, n)),
        pltpu.SemaphoreType.DMA((2, LAYERS, CHUNKS, n)),
        pltpu.SemaphoreType.DMA((2, LAYERS, CHUNKS, n)),
    ]
    result = pl.pallas_call(
        functools.partial(kernel, n, pn, cells),
        out_shape=jax.ShapeDtypeStruct((cells, LANES), f32),
        in_specs=[pl.BlockSpec(memory_space=pl.ANY)] * len(operands),
        out_specs=pl.BlockSpec(memory_space=pl.ANY),
        scratch_shapes=scratch,
        compiler_params=pltpu.CompilerParams(
            collective_id=0, has_side_effects=True, vmem_limit_bytes=60 * 1024 * 1024
        ),
    )(*operands)
    return result.reshape(cells_x, cells_y, LANES)


def solution(mesh):
    placed = (P(("groups", "gx"), "gy", None), P(None, "gx", None, "gy", None), P(), P())
    return jax.shard_map(
        shards,
        mesh=mesh,
        in_specs=placed,
        out_specs=P(("groups", "gx"), "gy", None),
        check_vma=False,
    )
```

time: 139 us -> 111 us (0.80)
  Pallas kernels: 127 us -> 107 us
  local copies, waits for them, and re-layouts: 10.5 us -> 3.16 us
    pallas_call x1, Pallas kernels: 127 us -> 107 us  [shards(): pl.pallas_call(functools.partial(kernel, n, pn, cells), out_shape=jax.Sha...]
    another operation x4 -> x0, local copies, waits for them, and re-layouts: 7.33 us -> none  [the longest x2 6.65 us: shards(): jnp.tile(mixing, (1, 16, 16))]
    unnamed x5 -> x1, local copies, waits for them, and re-layouts: 3.17 us -> 3.16 us
where the time goes in v2:
time: 111 us; the launch traced here: 110 us
  Pallas kernels  107 us (96%)
  local copies, waits for them, and re-layouts  3.16 us (3%)
    pallas_call x1, Pallas kernels, shards(): pl.pallas_call(functools.partial(kernel, n, pn, cells), out_shape=jax.Sha...  107 us
    unnamed x1, local copies, waits for them, and re-layouts  3.16 us

profile of v2, /device:TPU:0, one launch (start us, length us, event | category | flops | bytes accessed | tf_op | source)
XLA Modules:
  0.0 110.5 jit_solution(16950347924108241922)
XLA Ops:
  0.0 107.3 %shard_map.154 = f32[512,1024]{1,0:T(8,128)} custom-call(f32[512,1024]{1,0:T(8,128)} %bitcast.3, f32[2,4,2,16,8192]{4,3,2,1,0:T(8,128)} %refs_1_.1, f32[2,16,16]{2,1,0:T(8,128)} %refs_2_.1, f32[2,16]{1,0:T(2,128)} %refs_3_.1, bf16[2,1024,1024]{2,1,0:T(8,128)(2,1)} %constant.24.clone.refs_4_, bf16[2,2,256,512]{3,2,1,0:T(8,128)(2,1)} %constant.25.clone.refs_5_, ...), custom_call_target="tpu_custom_call" | custom-call | tf_op jit(solution)/shard_map/pallas_call | solution.py:449
  107.3 3.2 %copy.18 = f32[8,64,1024]{2,1,0:T(8,128)} copy(f32[8,64,1024]{2,1,0:T(8,128)} %bitcast.2) | data formatting | bytes 4194304

commit v3 on v2

--- a/solution.py
+++ b/solution.py
@@ -50,7 +50,8 @@
 def tables(n, pair_size, cells_x, cells_y):
     span_x, span_y = cells_x * n, cells_y * pair_size
     qs = MY // pair_size
-    qn, pn = qs // n, MX // n
+    group = n // 2
+    qn, pn = qs // group, MX // n
     eye = np.eye
     part_x = cells_x // HALVES
     cosine, sine = waves(np.arange(MZ), np.arange(NZ), NZ)
@@ -63,37 +64,37 @@
     y_forward, y_backward = [], []
     for g in range(pair_size):
         cosine, sine = waves(signed_modes(MY), g * cells_y + np.arange(cells_y), span_y)
-        forward = complex_rows(cosine, sine, -1).reshape(pair_size, n, qn, cells_y, 2, 2)
+        forward = complex_rows(cosine, sine, -1).reshape(pair_size, group, qn, cells_y, 2, 2)
         y_forward.append(
             pair(
                 np.einsum("hdqyab,xw->hdxqabwy", forward, eye(part_x)).reshape(
-                    pair_size * n * part_x * qn * 2, 2 * part_x * cells_y
+                    pair_size * group * part_x * qn * 2, 2 * part_x * cells_y
                 )
             )
         )
-        backward = complex_rows(cosine, sine, 1).reshape(pair_size, n, qn, cells_y, 2, 2)
+        backward = complex_rows(cosine, sine, 1).reshape(pair_size, group, qn, cells_y, 2, 2)
         y_backward.append(
             pair(
                 np.einsum("hdqyab,xw->awyhdxqb", backward, eye(part_x)).reshape(
-                    2 * part_x * cells_y, pair_size * n * part_x * qn * 2
+                    2 * part_x * cells_y, pair_size * group * part_x * qn * 2
                 )
             )
         )
     cosine, sine = waves(signed_modes(MX), np.arange(span_x), span_x)
     rows = pn * qn * 2
     padded = max(8, rows)
-    forward = complex_rows(cosine, sine, -1).reshape(n, pn, n, HALVES, part_x, 2, 2)
-    x_forward = np.einsum("dpshxab,qr->dpqahsxrb", forward, eye(qn)).reshape(n, rows, -1)
-    x_forward = np.pad(x_forward, ((0, 0), (0, padded - rows), (0, 0))).reshape(n * padded, -1)
-    backward = complex_rows(cosine, sine, 1).reshape(n, pn, n, HALVES, part_x, 2, 2)
-    x_backward = np.einsum("dpshxab,qr->hsxqadprb", backward, eye(qn)).reshape(-1, n, rows)
-    x_backward = np.pad(x_backward, ((0, 0), (0, 0), (0, padded - rows))).reshape(-1, n * padded)
-    order = np.zeros((pn, 2, n, qn, n, padded))
+    forward = complex_rows(cosine, sine, -1).reshape(n, pn, 2, group, HALVES, part_x, 2, 2)
+    x_forward = np.einsum("dpgshxab,qr->gdpqahsxrb", forward, eye(qn)).reshape(2, n, rows, -1)
+    x_forward = np.pad(x_forward, ((0, 0), (0, 0), (0, padded - rows), (0, 0))).reshape(2, n * padded, -1)
+    backward = complex_rows(cosine, sine, 1).reshape(n, pn, 2, group, HALVES, part_x, 2, 2)
+    x_backward = np.einsum("dpgshxab,qr->ghsxqadprb", backward, eye(qn)).reshape(2, HALVES * group * part_x * qn * 2, n, rows)
+    x_backward = np.pad(x_backward, ((0, 0), (0, 0), (0, 0), (0, padded - rows))).reshape(2, -1, n * padded)
+    order = np.zeros((pn, 2, group, qn, n, padded))
     for p in range(pn):
         for part in range(2):
             for s in range(n):
                 for q in range(qn):
-                    order[p, part, s, q, s, (p * qn + q) * 2 + part] = 1.0
+                    order[p, part, s % group, q, s, (p * qn + q) * 2 + part] = 1.0
     order = order.reshape(pn * 2 * qs, n * padded)
     spread = np.einsum("kl,cd,o->lckdo", eye(8), channels, np.ones(C)).reshape(128, 8, C * C)
     spread = np.concatenate([spread, spread]).transpose(1, 0, 2)
@@ -106,8 +107,8 @@
         zb=pair(z_backward),
         yf=np.stack(y_forward),
         yb=np.stack(y_backward),
-        xf=pair(x_forward),
-        xb=pair(x_backward),
+        xf=np.stack([pair(x_forward[g]) for g in range(2)]),
+        xb=np.stack([pair(x_backward[g]) for g in range(2)]),
         order=cast(order),
         back=cast(order.T),
         spread=cast(spread),
@@ -156,14 +157,21 @@
     core = lax.axis_index("gy")
     other = 1 - core
     rows_x = recv_1.shape[4]
-    quarter = n * rows_x
+    group = n // 2
+    mine = lax.rem(me, group)
+    base = me - mine
+    quarter = group * rows_x
     part_cells = cells // HALVES
     here = dict(field=signal, spectral=weights, mixing=mixing, bias=bias, zf=zf, yf=yf, xf=xf, order=order,
                 spread=spread, gather=gather, back=back, xb=xb, yb=yb, zb=zb, tile=tile, across=across)
     loads = {}
     for at, name in enumerate(("field", "zf", "yf", "xf", "order", "spread", "spectral", "gather", "back", "xb",
                                "yb", "mixing", "bias", "tile", "across", "zb")):
-        source = hbm[name].at[core] if name in ("yf", "yb") else hbm[name]
+        source = hbm[name]
+        if name in ("yf", "yb"):
+            source = source.at[core]
+        elif name in ("xf", "xb"):
+            source = source.at[me // group]
         loads[name] = pltpu.make_async_copy(source, here[name], load_sem.at[at])
         loads[name].start()
 
@@ -176,42 +184,42 @@
     lax.fori_loop(1, n, greet, 0)
     pl.semaphore_signal(barrier, inc=1, device_id={"gy": other}, device_id_type=MESH)
 
-    def copy_to(send, recv, sems, peer, slot):
+    def copy_to(send, recv, sems, first, peer, slot):
         return pltpu.make_async_remote_copy(
             src_ref=send.at[peer],
             dst_ref=recv.at[slot],
             send_sem=sems[0].at[peer],
             recv_sem=sems[1].at[slot],
-            device_id={"gx": peer},
+            device_id={"gx": first + peer},
             device_id_type=MESH,
         )
 
-    def exchange(send, recv, sems):
+    def exchange(send, recv, sems, first, own, size):
         def start(k, _):
-            peer = lax.rem(me + k, n)
-            copy_to(send, recv, sems, peer, me).start()
+            peer = lax.rem(own + k, size)
+            copy_to(send, recv, sems, first, peer, own).start()
             return 0
 
-        lax.fori_loop(1, n, start, 0)
-        recv[me] = send[me]
-
-    def arrive(send, recv, sems):
+        lax.fori_loop(1, size, start, 0)
+        recv[own] = send[own]
+
+    def arrive(send, recv, sems, first, own, size):
         def wait(k, _):
-            peer = lax.rem(me + k, n)
-            copy_to(send, recv, sems, peer, peer).wait()
+            peer = lax.rem(own + k, size)
+            copy_to(send, recv, sems, first, peer, peer).wait()
             return 0
 
-        lax.fori_loop(1, n, wait, 0)
+        lax.fori_loop(1, size, wait, 0)
 
     def outer(way, layer, j, h):
         sends, recvs = ((send_1, recv_1), (send_4, recv_4))[way]
         return (sends.at[layer, j, h], recvs.at[layer, j, h],
-                (outer_send.at[way, layer, j, h], outer_recv.at[way, layer, j, h]))
+                (outer_send.at[way, layer, j, h], outer_recv.at[way, layer, j, h]), base, mine, group)
 
     def inner(way, layer, j):
         sends, recvs = ((send_2, recv_2), (send_3, recv_3))[way]
         return (sends.at[layer, j], recvs.at[layer, j],
-                (inner_send.at[way, layer, j], inner_recv.at[way, layer, j]))
+                (inner_send.at[way, layer, j], inner_recv.at[way, layer, j]), 0, me, n)
 
     def pair_copy(way, layer, h, arriving=False):
         if way == 0:
@@ -251,7 +259,7 @@
         for j in range(CHUNKS):
             lanes = slice(j * CW, (j + 1) * CW)
             value = send_y[layer, h, core, :, lanes] + recv_y[layer, h, :, lanes]
-            send_1[layer, j, h] = value.reshape(n, rows_x, CW)
+            send_1[layer, j, h] = value.reshape(group, rows_x, CW)
             exchange(*outer(0, layer, j, h))
 
     def x_forward(layer, j):
@@ -264,8 +272,7 @@
     def mix(layer, j):
         arrive(*inner(0, layer, j))
         high, low = split(recv_2[layer, j].reshape(order.shape[1], CW))
-        high = dot(order[...], high).astype(jnp.bfloat16)
-        low = dot(order[...], low).astype(jnp.bfloat16)
+        high, low = split(dot(order[...], high) + dot(order[...], low))
         kept = order.shape[0]
         left = jnp.concatenate(
             [
@@ -408,8 +415,9 @@
     table = tables(n, pair_size, cells_x, cells_y)
     pn = spectral.shape[1]
     qs = spectral.shape[3]
-    rows_x = cells_x // HALVES * (qs // n) * 2
-    rows_p = table["xf"].shape[1] // n
+    group = n // 2
+    rows_x = cells_x // HALVES * (qs // group) * 2
+    rows_p = table["xf"].shape[2] // n
     operands = [field.reshape(cells, LANES), spectral, mixing, bias] + [
         jnp.asarray(table[name])
         for name in ("zf", "yf", "xf", "order", "spread", "gather", "back", "xb", "yb", "zb", "tile", "across")
@@ -417,9 +425,9 @@
     f32, bf16 = jnp.float32, jnp.bfloat16
     scratch = []
     for at, operand in enumerate(operands):
-        shape = operand.shape[1:] if at in (5, 12) else operand.shape
+        shape = operand.shape[1:] if at in (5, 6, 11, 12) else operand.shape
         scratch.append(pltpu.VMEM(shape, operand.dtype))
-    quarter = n * rows_x
+    quarter = group * rows_x
     kept = pn * 2 * qs
     part_cells = cells // HALVES
     scratch += [pltpu.VMEM((cells, LANES), bf16)] * 2
@@ -433,7 +441,7 @@
         pltpu.VMEM((LAYERS, HALVES, 2, quarter, WIDTH), f32),
         pltpu.VMEM((LAYERS, HALVES, quarter, WIDTH), f32),
     ]
-    for shape in ((HALVES, n, rows_x), (n, rows_p), (n, rows_p), (HALVES, n, rows_x)):
+    for shape in ((HALVES, group, rows_x), (n, rows_p), (n, rows_p), (HALVES, group, rows_x)):
         scratch += [pltpu.VMEM((LAYERS, CHUNKS) + shape + (CW,), f32)] * 2
     scratch += [
         pltpu.VMEM((LAYERS, HALVES, 2, quarter, WIDTH), f32),
@@ -441,8 +449,8 @@
         pltpu.SemaphoreType.DMA,
         pltpu.SemaphoreType.DMA((2, LAYERS, HALVES)),
         pltpu.SemaphoreType.DMA((2, LAYERS, HALVES)),
-        pltpu.SemaphoreType.DMA((2, LAYERS, CHUNKS, HALVES, n)),
-        pltpu.SemaphoreType.DMA((2, LAYERS, CHUNKS, HALVES, n)),
+        pltpu.SemaphoreType.DMA((2, LAYERS, CHUNKS, HALVES, group)),
+        pltpu.SemaphoreType.DMA((2, LAYERS, CHUNKS, HALVES, group)),
         pltpu.SemaphoreType.DMA((2, LAYERS, CHUNKS, n)),
         pltpu.SemaphoreType.DMA((2, LAYERS, CHUNKS, n)),
     ]

time: 111 us -> 112 us (level)
  Pallas kernels: 107 us -> 109 us
    pallas_call x1, Pallas kernels: 107 us -> 109 us  [shards(): pl.pallas_call(functools.partial(kernel, n, pn, cells), out_shape=jax.Sha...]
where the time goes in v3:
time: 112 us
  Pallas kernels  109 us (97%)
  local copies, waits for them, and re-layouts  3.16 us (3%)
    pallas_call x1, Pallas kernels, shards(): pl.pallas_call(functools.partial(kernel, n, pn, cells), out_shape=jax.Sha...  109 us
    unnamed x1, local copies, waits for them, and re-layouts  3.16 us

profile of v3, /device:TPU:0, one launch (start us, length us, event | category | flops | bytes accessed | tf_op | source)
XLA Modules:
  0.0 112.0 jit_solution(2813177828765099051)
XLA Ops:
  0.0 108.9 %shard_map.154 = f32[512,1024]{1,0:T(8,128)} custom-call(f32[512,1024]{1,0:T(8,128)} %bitcast.3, f32[2,4,2,16,8192]{4,3,2,1,0:T(8,128)} %refs_1_.1, f32[2,16,16]{2,1,0:T(8,128)} %refs_2_.1, f32[2,16]{1,0:T(2,128)} %refs_3_.1, bf16[2,1024,1024]{2,1,0:T(8,128)(2,1)} %constant.24.clone.refs_4_, bf16[2,2,256,512]{3,2,1,0:T(8,128)(2,1)} %constant.25.clone.refs_5_, ...), custom_call_target="tpu_custom_call" | custom-call | tf_op jit(solution)/shard_map/pallas_call | solution.py:457
  108.9 3.2 %copy.18 = f32[8,64,1024]{2,1,0:T(8,128)} copy(f32[8,64,1024]{2,1,0:T(8,128)} %bitcast.2) | data formatting | bytes 4194304
